TPU v7x, 1024 devices: a whole 4x8x16 slice. The times are simulated.
1024 devices in a mesh: dp: 64 (over x, y, core), mp: 16 (over z).
Axes of the slice: x: 4, y: 8, z: 16, core: 2. Of those that a mesh axis runs over, the one named last changes fastest.
Arguments:
- statistics: bfloat16 [128, 8192, 512], P('dp', 'mp'), as said below
- gradients: bfloat16 [128, 16, 512, 512], P('dp', None, 'mp'), may hold values from -6 to 6
- counts: int32 [64], P('dp'), may hold values from 0 to 2, as said below
Outputs:
- preconditioned: bfloat16 [128, 16, 512, 512], P('dp', None, 'mp')
Inputs may be any that keep to these rules, and one draw needn't show every extreme that they name: counts[2 i] + counts[2 i + 1] == 2 for every i < 32, and some owner has 2. `statistics`: each statistic block is symmetric positive definite.
All inputs are finite; a program needn't handle non-finite values.
Results may differ from a plain program's by a relative error of at most 0.0067.
Values may be sent and summed in bfloat16 or wider, within the bound.
A program may use at most 32 MiB of HBM per device.

v0:
```python
import jax
import jax.numpy as jnp
from jax import lax
from jax.sharding import PartitionSpec as P


def newton(blocks):
    order = blocks.shape[-1]
    values = blocks.astype(jnp.float32)
    norm_scale = jnp.sqrt(jnp.sum(values * values, axis=(1, 2))) + 1e-06
    scaled = (values / norm_scale[:, None, None]).astype(jnp.bfloat16)
    identity = jnp.eye(order, dtype=jnp.float32)
    step_one = ((5.0 * identity - scaled.astype(jnp.float32)) * 0.25).astype(jnp.bfloat16)
    square = jnp.einsum(
        "nij,njk->nik", step_one, step_one, preferred_element_type=jnp.float32
    ).astype(jnp.bfloat16)
    fourth = jnp.einsum("nij,njk->nik", square, square, preferred_element_type=jnp.float32).astype(
        jnp.bfloat16
    )
    updated = jnp.einsum("nij,njk->nik", fourth, scaled, preferred_element_type=jnp.float32)
    step_two = ((5.0 * identity - updated) * 0.25).astype(jnp.bfloat16)
    product = jnp.einsum("nij,njk->nik", step_one, step_two, preferred_element_type=jnp.float32)
    return (product * (norm_scale ** (-0.25))[:, None, None]).astype(jnp.bfloat16)


def on_device(statistics, gradients, counts):
    slots = statistics.shape[0]
    live_count = counts[0]
    columns = lax.all_to_all(gradients, "mp", split_axis=1, concat_axis=2, tiled=True)
    inv_roots = newton(statistics)
    product = jnp.einsum(
        "skj,sij->ski", columns[:, 0], inv_roots, preferred_element_type=jnp.float32
    )
    keep_slot = (jnp.arange(slots) < live_count)[:, None, None]
    product = jnp.where(keep_slot, product, 0.0).astype(jnp.bfloat16)
    return lax.all_to_all(product[:, None], "mp", split_axis=2, concat_axis=1, tiled=True)


def solution(mesh):
    in_specs = (P("dp", "mp", None), P("dp", None, "mp", None), P("dp"))
    out_specs = P("dp", None, "mp", None)
    return jax.shard_map(
        on_device, mesh=mesh, in_specs=in_specs, out_specs=out_specs, check_vma=False
    )
```

profile of v0, /device:TPU:20, one launch (start us, length us, event | category | flops | bytes accessed | tf_op | source)
XLA Modules:
  0.0 133.6 jit_solution(10368877886755127364)
XLA Ops:
  0.0 2.4 %copy.6 = bf16[2,16,32,512]{3,2,0,1:T(8,128)(2,1)} copy(bf16[2,16,32,512]{3,2,1,0:T(8,128)(2,1)} %param.4) | data formatting | bytes 2097152 | tf_op args[1]
  2.4 18.9 %all-to-all-start = ((bf16[2,16,32,512]{3,2,0,1:T(8,128)(2,1)}), bf16[2,16,32,512]{3,2,0,1:T(8,128)(2,1)S(1)}, u32[]{:S(2)}, u32[]{:S(2)}) async-start(bf16[2,16,32,512]{3,2,0,1:T(8,128)(2,1)} %copy.6), calls=%async_computation | async-start | bytes 2097152 | tf_op jit(solution)/shard_map/all_to_all | solution.py:29
  21.2 0.0 copy-start
  22.0 0.1 fusion.7
  22.1 0.4 copy-done
  22.5 0.4 fusion
  22.9 3.3 %convolution_convert_fusion = bf16[2,512,512]{2,1,0:T(8,128)(2,1)} fusion(f32[512,512]{1,0:T(8,128)S(1)} %fusion.7, bf16[2,512,512]{2,1,0:T(8,128)(2,1)S(1)} %copy-done, f32[2]{0:T(128)S(1)} %get-tuple-element.6), kind=kOutput, calls=%fused_computation.8 | convolution fusion | flops 1078460416 | bytes 3145736 | tf_op jit(solution)/shard_map/nij,njk->nik/dot_general | solution.py:17
  26.2 3.7 %multiply_convert_fusion = bf16[2,512,512]{2,1,0:T(8,128)(2,1)} fusion(bf16[2,512,512]{2,1,0:T(8,128)(2,1)} %convolution_convert_fusion, f32[2]{0:T(128)S(1)} %get-tuple-element.5, f32[512,512]{1,0:T(8,128)S(1)} %fusion.7, bf16[2,512,512]{2,1,0:T(8,128)(2,1)S(1)} %copy-done, f32[2]{0:T(128)S(1)} %get-tuple-element.6), kind=kOutput, calls=%fused_computation.5 | convolution fusion | flops 1081606144 | bytes 4194320 | tf_op jit(solution)/shard_map/nij,njk->nik/dot_general | solution.py:22
  29.9 0.0 copy-start.1
  29.9 41.3 %all-to-all-done = bf16[2,16,32,512]{3,2,0,1:T(8,128)(2,1)S(1)} async-done(((bf16[2,16,32,512]{3,2,0,1:T(8,128)(2,1)}), bf16[2,16,32,512]{3,2,0,1:T(8,128)(2,1)S(1)}, u32[]{:S(2)}, u32[]{:S(2)}) %all-to-all-start) | async-done | bytes 1048608 | tf_op jit(solution)/shard_map/all_to_all | solution.py:29
  71.2 0.1 copy.7
  71.3 0.0 copy-done.1
  71.3 0.7 fusion.2
  72.0 1.0 copy.8
  73.0 59.5 %all_to_all.21 = bf16[2,1,512,512]{3,0,1,2:T(2,128)(2,1)S(1)} all-to-all(bf16[2,1,512,512]{3,0,1,2:T(2,128)(2,1)S(1)} %copy.8), channel_id=1, replica_groups=mesh['dp'=64,'mp'=16] {'mp'}, dimensions={2} | all-to-all | bytes 2097152 | tf_op jit(solution)/shard_map/all_to_all | solution.py:36
  132.5 1.1 copy.9
  (2 shorter events, 0.0 us)
Async XLA Ops:
  2.4 68.8 %all-to-all-start = ((bf16[2,16,32,512]{3,2,0,1:T(8,128)(2,1)}), bf16[2,16,32,512]{3,2,0,1:T(8,128)(2,1)S(1)}, u32[]{:S(2)}, u32[]{:S(2)}) async-start(bf16[2,16,32,512]{3,2,0,1:T(8,128)(2,1)} %copy.6), calls=%async_computation | async-start | bytes 2097152 | tf_op jit(solution)/shard_map/all_to_all | solution.py:29
  21.2 1.2 copy-start
  29.9 41.4 %copy-start.1 = (bf16[2,512,512]{2,1,0:T(8,128)(2,1)S(1)}, bf16[2,512,512]{2,1,0:T(8,128)(2,1)}, u32[]{:S(2)}) copy-start(bf16[2,512,512]{2,1,0:T(8,128)(2,1)} %multiply_convert_fusion) | copy-start | bytes 3145732
where the time goes:
time: 134 us
  blocking collectives  59.5 us (44%)
  waiting for transfers between devices  41.3 us (31%)
  starting transfers between devices  18.9 us (14%)
  matrix products  7.74 us (6%)
  local copies, waits for them, and re-layouts  4.91 us (4%)
    all_to_all x1, blocking collectives, on_device(): lax.all_to_all(product[:, None], 'mp', split_axis=2, concat_axis=1, tiled...  59.5 us
    all_to_all x1, waiting for transfers between devices, on_device(): lax.all_to_all(gradients, 'mp', split_axis=1, concat_axis=2, tiled=True)  41.3 us
    all_to_all x1, starting transfers between devices, on_device(): lax.all_to_all(gradients, 'mp', split_axis=1, concat_axis=2, tiled=True)  18.9 us
    dot_general x1, matrix products, newton(): jnp.einsum('nij,njk->nik', step_one, step_two, preferred_element_type=jnp...  3.67 us
    dot_general x1, matrix products, newton(): jnp.einsum('nij,njk->nik', square, square, preferred_element_type=jnp.flo...  3.33 us
    unnamed x5, local copies, waits for them, and re-layouts  2.73 us
  transfers between devices with their start and end apart: 1, of which 1 were waited for; matrix products, arithmetic and copies ran while one was open for 6% of the time, Pallas kernels for 0%

commit v1 on v0

--- a/solution.py
+++ b/solution.py
@@ -1,3 +1,4 @@
+import functools
 import jax
 import jax.numpy as jnp
 from jax import lax
@@ -23,22 +24,37 @@
     return (product * (norm_scale ** (-0.25))[:, None, None]).astype(jnp.bfloat16)
 
 
-def on_device(statistics, gradients, counts):
-    slots = statistics.shape[0]
-    live_count = counts[0]
-    columns = lax.all_to_all(gradients, "mp", split_axis=1, concat_axis=2, tiled=True)
-    inv_roots = newton(statistics)
+def sibling(mesh, value):
+    size = mesh.shape["dp"]
+    return lax.ppermute(value, "dp", [(at, at ^ 1) for at in range(size)])
+
+
+def on_device(mesh, statistics, gradients, counts):
+    count = counts[0]
+    order = statistics.shape[2]
+    own_first = count >= 1
+    block = jnp.where(own_first, statistics[0], sibling(mesh, statistics[1]))
+    rows = jnp.where(own_first, gradients[0], sibling(mesh, gradients[1]))
+    columns = lax.all_to_all(rows, "mp", split_axis=0, concat_axis=1, tiled=True)
+    inv_root = newton(block.reshape(1, order, order))[0]
     product = jnp.einsum(
-        "skj,sij->ski", columns[:, 0], inv_roots, preferred_element_type=jnp.float32
-    )
-    keep_slot = (jnp.arange(slots) < live_count)[:, None, None]
-    product = jnp.where(keep_slot, product, 0.0).astype(jnp.bfloat16)
-    return lax.all_to_all(product[:, None], "mp", split_axis=2, concat_axis=1, tiled=True)
+        "kj,ij->ki", columns[0], inv_root, preferred_element_type=jnp.float32
+    ).astype(jnp.bfloat16)
+    result = lax.all_to_all(product[None], "mp", split_axis=1, concat_axis=0, tiled=True)
+    other = sibling(mesh, result)
+    zero = jnp.zeros_like(result)
+    first = jnp.where(own_first, result, zero)
+    second = jnp.where(count >= 2, other, zero)
+    return jnp.stack([first, second])
 
 
 def solution(mesh):
     in_specs = (P("dp", "mp", None), P("dp", None, "mp", None), P("dp"))
     out_specs = P("dp", None, "mp", None)
     return jax.shard_map(
-        on_device, mesh=mesh, in_specs=in_specs, out_specs=out_specs, check_vma=False
+        functools.partial(on_device, mesh),
+        mesh=mesh,
+        in_specs=in_specs,
+        out_specs=out_specs,
+        check_vma=False,
     )

time: 134 us -> 102 us (0.76)
  the two profiles are of different devices: /device:TPU:20 before, /device:TPU:1 now
where the time goes in v1:
time: 102 us
  blocking collectives  35.5 us (35%)
  starting transfers between devices  33.6 us (33%)
  waiting for transfers between devices  18.6 us (18%)
  other arithmetic  6.75 us (7%)
  local copies, waits for them, and re-layouts  3.43 us (3%)
  matrix products  2.74 us (3%)
  between operations  1.48 us (1%)
    all_to_all x1, blocking collectives, on_device(): lax.all_to_all(product[None], 'mp', split_axis=1, concat_axis=0, tiled=True)  35.5 us
    ppermute x3, starting transfers between devices, sibling(): return lax.ppermute(value, 'dp', [(at, at ^ 1) for at in range(size)])  27.6 us
    all_to_all x1, waiting for transfers between devices, on_device(): lax.all_to_all(rows, 'mp', split_axis=0, concat_axis=1, tiled=True)  14.7 us
    all_to_all x1, starting transfers between devices, on_device(): lax.all_to_all(rows, 'mp', split_axis=0, concat_axis=1, tiled=True)  5.93 us
    ppermute x3, waiting for transfers between devices, sibling(): return lax.ppermute(value, 'dp', [(at, at ^ 1) for at in range(size)])  3.89 us
    unnamed x1, other arithmetic  3.82 us
  transfers between devices with their start and end apart: 4, of which 4 were waited for; matrix products, arithmetic and copies ran while one was open for 3% of the time, Pallas kernels for 0%

profile of v1, /device:TPU:1, one launch (start us, length us, event | category | flops | bytes accessed | tf_op | source)
XLA Modules:
  0.0 102.1 jit_solution(10326094280672434747)
XLA Ops:
  0.0 0.0 copy-start.1
  0.0 1.2 %slice_bitcast_fusion.1 = bf16[16,32,512]{2,1,0:T(8,128)(2,1)S(1)} fusion(bf16[2,16,32,512]{3,2,1,0:T(8,128)(2,1)} %param.4), kind=kLoop, calls=%fused_computation.28 | loop fusion | bytes 1048576 | tf_op jit(solution)/shard_map/squeeze | solution.py:37
  1.2 16.1 %collective-permute-start = (bf16[16,32,512]{2,1,0:T(8,128)(2,1)S(1)}, bf16[16,32,512]{2,1,0:T(8,128)(2,1)S(1)}, u32[]{:S(2)}, u32[]{:S(2)}) collective-permute-start(bf16[16,32,512]{2,1,0:T(8,128)(2,1)S(1)} %slice_bitcast_fusion.1), channel_id=1, source_target_pairs={{0,16},{16,0},{32,48},{48,32},{64,80},{80,64},{96,112},{112,96},{1... | collective-permute-start | bytes 1572872 | tf_op jit(solution)/shard_map/ppermute | solution.py:29
  17.9 0.9 collective-permute-done
  18.8 0.0 copy-done.1
  18.8 0.0 copy-start
  18.8 0.8 bitcast_select_fusion.1
  19.6 5.9 %all-to-all-start = ((bf16[16,32,512]{2,1,0:T(8,128)(2,1)}), bf16[16,32,512]{2,1,0:T(8,128)(2,1)S(1)}, u32[]{:S(2)}, u32[]{:S(2)}) async-start(bf16[16,32,512]{2,1,0:T(8,128)(2,1)} %bitcast_select_fusion.1), calls=%async_computation | async-start | bytes 1048576 | tf_op jit(solution)/shard_map/all_to_all | solution.py:38
  25.6 0.0 copy-done
  25.6 2.6 %collective-permute-start.1 = (bf16[512,512]{1,0:T(8,128)(2,1)S(1)}, bf16[512,512]{1,0:T(8,128)(2,1)S(1)}, u32[]{:S(2)}, u32[]{:S(2)}) collective-permute-start(bf16[512,512]{1,0:T(8,128)(2,1)S(1)} %slice_bitcast_fusion), channel_id=1, source_target_pairs={{0,16},{16,0},{32,48},{48,32},{64,80},{80,64},{96,112},{112,96},{1... | collective-permute-start | bytes 1572872 | tf_op jit(solution)/shard_map/ppermute | solution.py:29
  28.2 1.5 %collective-permute-done.1 = bf16[512,512]{1,0:T(8,128)(2,1)S(1)} collective-permute-done((bf16[512,512]{1,0:T(8,128)(2,1)S(1)}, bf16[512,512]{1,0:T(8,128)(2,1)S(1)}, u32[]{:S(2)}, u32[]{:S(2)}) %collective-permute-start.1) | collective-permute-done | bytes 524320 | tf_op jit(solution)/shard_map/ppermute | solution.py:29
  29.7 0.9 fusion.4
  31.3 1.4 %convolution_convert_fusion.1 = bf16[512,512]{1,0:T(8,128)(2,1)S(1)} fusion(f32[]{:T(128)S(6)} %add.4, bf16[512,512]{1,0:T(8,128)(2,1)S(1)} %collective-permute-done.1, bf16[2,512,512]{2,1,0:T(8,128)(2,1)S(1)} %copy-done, pred[]{:T(512)} %bitcast), kind=kOutput, calls=%fused_computation.7 | convolution fusion | flops 540016640 | bytes 1572869 | tf_op jit(solution)/shard_map/nij,njk->nik/dot_general | solution.py:18
  32.7 0.9 fusion.2
  33.6 14.7 %all-to-all-done = bf16[16,32,512]{2,1,0:T(8,128)(2,1)S(1)} async-done(((bf16[16,32,512]{2,1,0:T(8,128)(2,1)}), bf16[16,32,512]{2,1,0:T(8,128)(2,1)S(1)}, u32[]{:S(2)}, u32[]{:S(2)}) %all-to-all-start) | async-done | bytes 524320 | tf_op jit(solution)/shard_map/all_to_all | solution.py:38
  48.3 0.5 fusion.3
  48.8 0.8 copy.10
  49.6 0.5 broadcast.71
  50.1 3.8 %reduce.2 = bf16[512,512]{1,0:T(8,128)(2,1)S(1)} reduce(bf16[512,1,512]{2,1,0:T(2,128)(2,1)S(1)} %bitcast.37, bf16[]{:T(256)} %broadcast.71), dimensions={1}, to_apply=%bitcast.35.reduce_sub_computation | reduce | bytes 1048578
  53.9 0.4 reshape.75
  54.3 35.5 %all_to_all.21 = bf16[16,2,8192]{2,1,0:T(2,128)(2,1)S(1)} all-to-all(bf16[16,2,8192]{2,1,0:T(2,128)(2,1)S(1)} %reshape.75), channel_id=1, replica_groups=mesh['dp'=64,'mp'=16] {'mp'}, dimensions={0} | all-to-all | bytes 1048576 | tf_op jit(solution)/shard_map/all_to_all | solution.py:43
  89.8 0.5 reshape.76
  90.3 0.1 broadcast_select_fusion
  90.4 9.0 %collective-permute-start.2 = (bf16[16,32,512]{2,1,0:T(8,128)(2,1)S(1)}, bf16[16,32,512]{2,1,0:T(8,128)(2,1)S(1)}, u32[]{:S(2)}, u32[]{:S(2)}) collective-permute-start(bf16[16,32,512]{2,1,0:T(8,128)(2,1)S(1)} %bitcast.40), channel_id=1, source_target_pairs={{0,16},{16,0},{32,48},{48,32},{64,80},{80,64},{96,112},{112,96},{1... | collective-permute-start | bytes 1572872 | tf_op jit(solution)/shard_map/ppermute | solution.py:29
  99.4 1.5 %collective-permute-done.2 = bf16[16,32,512]{2,1,0:T(8,128)(2,1)S(1)} collective-permute-done((bf16[16,32,512]{2,1,0:T(8,128)(2,1)S(1)}, bf16[16,32,512]{2,1,0:T(8,128)(2,1)S(1)}, u32[]{:S(2)}, u32[]{:S(2)}) %collective-permute-start.2) | collective-permute-done | bytes 524320 | tf_op jit(solution)/shard_map/ppermute | solution.py:29
  101.0 1.1 %pad_maximum_fusion = bf16[2,16,32,512]{3,2,1,0:T(8,128)(2,1)} fusion(bf16[1,16,32,512]{3,2,1,0:T(8,128)(2,1)S(1)} %select_bitcast_fusion, bf16[1,16,32,512]{3,2,1,0:T(8,128)(2,1)S(1)} %bitcast.39), kind=kLoop, calls=%fused_computation.16 | loop fusion | flops 524288 | bytes 2097152 | tf_op jit(solution)/shard_map/stack | solution.py:48
  (2 shorter events, 0.1 us)
Async XLA Ops:
  0.0 18.8 %copy-start.1 = (bf16[2,16,32,512]{3,2,1,0:T(8,128)(2,1)S(1)}, bf16[2,16,32,512]{3,2,1,0:T(8,128)(2,1)}, u32[]{:S(2)}) copy-start(bf16[2,16,32,512]{3,2,1,0:T(8,128)(2,1)} %param.4) | copy-start | bytes 3145732
  1.2 17.6 %collective-permute-start = (bf16[16,32,512]{2,1,0:T(8,128)(2,1)S(1)}, bf16[16,32,512]{2,1,0:T(8,128)(2,1)S(1)}, u32[]{:S(2)}, u32[]{:S(2)}) collective-permute-start(bf16[16,32,512]{2,1,0:T(8,128)(2,1)S(1)} %slice_bitcast_fusion.1), channel_id=1, source_target_pairs={{0,16},{16,0},{32,48},{48,32},{64,80},{80,64},{96,112},{112,96},{1... | collective-permute-start | bytes 1572872 | tf_op jit(solution)/shard_map/ppermute | solution.py:29
  18.8 6.8 %copy-start = (bf16[2,512,512]{2,1,0:T(8,128)(2,1)S(1)}, bf16[2,512,512]{2,1,0:T(8,128)(2,1)}, u32[]{:S(2)}) copy-start(bf16[2,512,512]{2,1,0:T(8,128)(2,1)} %param.3) | copy-start | bytes 3145732
  19.6 28.7 %all-to-all-start = ((bf16[16,32,512]{2,1,0:T(8,128)(2,1)}), bf16[16,32,512]{2,1,0:T(8,128)(2,1)S(1)}, u32[]{:S(2)}, u32[]{:S(2)}) async-start(bf16[16,32,512]{2,1,0:T(8,128)(2,1)} %bitcast_select_fusion.1), calls=%async_computation | async-start | bytes 1048576 | tf_op jit(solution)/shard_map/all_to_all | solution.py:38
  25.6 4.1 %collective-permute-start.1 = (bf16[512,512]{1,0:T(8,128)(2,1)S(1)}, bf16[512,512]{1,0:T(8,128)(2,1)S(1)}, u32[]{:S(2)}, u32[]{:S(2)}) collective-permute-start(bf16[512,512]{1,0:T(8,128)(2,1)S(1)} %slice_bitcast_fusion), channel_id=1, source_target_pairs={{0,16},{16,0},{32,48},{48,32},{64,80},{80,64},{96,112},{112,96},{1... | collective-permute-start | bytes 1572872 | tf_op jit(solution)/shard_map/ppermute | solution.py:29
  90.4 10.5 %collective-permute-start.2 = (bf16[16,32,512]{2,1,0:T(8,128)(2,1)S(1)}, bf16[16,32,512]{2,1,0:T(8,128)(2,1)S(1)}, u32[]{:S(2)}, u32[]{:S(2)}) collective-permute-start(bf16[16,32,512]{2,1,0:T(8,128)(2,1)S(1)} %bitcast.40), channel_id=1, source_target_pairs={{0,16},{16,0},{32,48},{48,32},{64,80},{80,64},{96,112},{112,96},{1... | collective-permute-start | bytes 1572872 | tf_op jit(solution)/shard_map/ppermute | solution.py:29

commit v2 on v0

v2 whole, which is shorter than its diff:
```python
import functools

import jax
import jax.numpy as jnp
from jax import lax
from jax.experimental import pallas as pl
from jax.experimental.pallas import tpu as pltpu
from jax.sharding import PartitionSpec as P

MESH = pl.DeviceIdType.MESH
LANES = 128
TAIL = 16
F32 = jnp.float32
BF16 = jnp.bfloat16


def dot(a, b):
    return jnp.dot(a, b, preferred_element_type=F32)


def dot_t(a, b):
    return lax.dot_general(a, b, (((1,), (1,)), ((), ())), preferred_element_type=F32)


def iotas(shape):
    return lax.broadcasted_iota(jnp.int32, shape, 0), lax.broadcasted_iota(jnp.int32, shape, 1)


def newton_root(block):
    order = block.shape[0]
    values = block.astype(F32)
    total = jnp.sum(jnp.sum(values * values, axis=1, keepdims=True), axis=0, keepdims=True)
    norm_scale = jnp.sqrt(total) + 1e-06
    scaled = (values * (1.0 / norm_scale)).astype(BF16)
    row, column = iotas((order, order))
    five = jnp.where(row == column, 5.0, 0.0).astype(F32)
    step_one = ((five - scaled.astype(F32)) * 0.25).astype(BF16)
    square = dot(step_one, step_one).astype(BF16)
    fourth = dot(square, square).astype(BF16)
    updated = dot(fourth, scaled)
    step_two = ((five - updated) * 0.25).astype(BF16)
    return dot(step_one, step_two) * lax.rsqrt(jnp.sqrt(norm_scale))


def pack(root, ref):
    half = root.shape[0] // 2
    slabs = half // LANES
    row, column = iotas((half, half))
    corner = root[half:, half:]
    across = root[:half, half:].astype(BF16)
    both = jnp.where(row <= column, root[:half, :half], corner).astype(BF16)
    diagonal = jnp.sum(jnp.where(row == column, corner, 0.0), axis=0, keepdims=True)
    tail_row, _ = iotas((TAIL, LANES))
    tail = jnp.zeros((TAIL, LANES), F32)
    for j in range(slabs):
        lanes = slice(j * LANES, (j + 1) * LANES)
        ref[j * half : (j + 1) * half, :] = across[:, lanes]
        ref[(slabs + j) * half : (slabs + j + 1) * half, :] = both[:, lanes]
        tail = jnp.where(tail_row == j, diagonal[:, lanes], tail)
    ref[2 * slabs * half :, :] = tail.astype(BF16)


def unpack(ref, half):
    slabs = half // LANES
    row, column = iotas((half, half))
    across = jnp.concatenate([ref[j * half : (j + 1) * half, :] for j in range(slabs)], axis=1)
    both = jnp.concatenate(
        [ref[(slabs + j) * half : (slabs + j + 1) * half, :] for j in range(slabs)], axis=1
    ).astype(F32)
    tail = ref[2 * slabs * half :, :].astype(F32)
    diagonal = jnp.concatenate([tail[j : j + 1, :] for j in range(slabs)], axis=1)
    mirror = both.T
    first = jnp.where(row <= column, both, mirror).astype(BF16)
    last = jnp.where(row > column, both, jnp.where(row == column, diagonal, mirror)).astype(BF16)
    return first, across, last


def apply_root(rows, ref):
    half = rows.shape[1] // 2
    first, across, last = unpack(ref, half)
    left, right = rows[:, :half], rows[:, half:]
    out_left = dot(left, first) + dot_t(right, across)
    out_right = dot(left, across) + dot(right, last)
    return jnp.concatenate([out_left, out_right], axis=1).astype(BF16)


def kernel(
    ring,
    reach,
    counts_ref,
    stat_ref,
    grad_ref,
    out_ref,
    stat_own,
    stat_sib,
    grad_own,
    grad_sib,
    grad_sel,
    request,
    answer,
    own_root,
    roots,
    result,
    local_sem,
    sib_send,
    sib_recv,
    row_send,
    row_recv,
    root_send,
    root_recv,
    back_send,
    back_recv,
    out_local,
    out_send,
    out_recv,
):
    dp, me = lax.axis_index("dp"), lax.axis_index("mp")
    core = lax.rem(dp, 2)
    sibling = {"dp": dp + 1 - 2 * core}
    sign = 1 - 2 * core
    order = stat_own.shape[0]
    half = order // 2
    chunks = 2 * half // LANES
    height = grad_own.shape[1]

    def at(offset):
        return lax.rem(me + sign * offset + 4 * ring, ring)

    def to(offset):
        return {"mp": at(offset)}

    stat_copy = pltpu.make_async_copy(stat_ref.at[0], stat_own, local_sem.at[0])
    grad_copy = pltpu.make_async_copy(grad_ref.at[0], grad_own, local_sem.at[1])
    grad_copy.start()
    stat_copy.start()

    barrier = pltpu.get_barrier_semaphore()
    pl.semaphore_signal(barrier, inc=1, device_id=sibling, device_id_type=MESH)
    for d in range(1, reach + 1):
        pl.semaphore_signal(barrier, inc=1, device_id=to(d), device_id_type=MESH)
        pl.semaphore_signal(barrier, inc=1, device_id=to(-d), device_id_type=MESH)
    pl.semaphore_wait(barrier, 2 * reach + 1)

    def far_first(j):
        return lax.rem(me + reach + 1 + j, ring)

    def grad_swap(j):
        block = far_first(j)
        return pltpu.make_async_remote_copy(
            src_ref=grad_ref.at[1, block],
            dst_ref=grad_sib.at[block],
            send_sem=sib_send.at[j],
            recv_sem=sib_recv.at[j],
            device_id=sibling,
            device_id_type=MESH,
        )

    stat_swap = pltpu.make_async_remote_copy(
        src_ref=stat_ref.at[1],
        dst_ref=stat_sib,
        send_sem=sib_send.at[ring],
        recv_sem=sib_recv.at[ring],
        device_id=sibling,
        device_id_type=MESH,
    )
    far = ring - 2 * reach - 1
    for j in range(far):
        grad_swap(j).start()
    stat_swap.start()
    for j in range(far, ring):
        grad_swap(j).start()

    own_first = counts_ref[0] >= 1

    def select_rows(j):
        grad_swap(j).wait_recv()
        block = far_first(j)
        grad_sel[block] = jnp.where(own_first, grad_own[block], grad_sib[block])

    grad_copy.wait()
    far_sides = [(1, k) for k in range(1, ring // 2 - reach + 1)]
    far_sides += [(0, k) for k in range(1, ring // 2 - reach)]

    def row_copy(side, k):
        way = 1 if side else -1
        return pltpu.make_async_remote_copy(
            src_ref=grad_sel.at[at(way * (reach + k))],
            dst_ref=request.at[side, pl.ds(k * height, height)],
            send_sem=row_send.at[side, k],
            recv_sem=row_recv.at[side, k],
            device_id=to(way * k),
            device_id_type=MESH,
        )

    for j in range(far):
        select_rows(j)
    for side, k in far_sides:
        row_copy(side, k).start()

    stat_copy.wait()
    stat_swap.wait_recv()
    pack(newton_root(jnp.where(own_first, stat_own[...], stat_sib[...])), own_root)

    def piece(c):
        return pl.ds(c * half, half if c < chunks - 1 else half + TAIL)

    def root_copy(side, d, c):
        source = own_root if d == 1 else roots.at[side, d - 2]
        return pltpu.make_async_remote_copy(
            src_ref=source.at[piece(c)],
            dst_ref=roots.at[side, d - 1, piece(c)],
            send_sem=root_send.at[side, d - 1, c],
            recv_sem=root_recv.at[side, d - 1, c],
            device_id=to(-1 if side else 1),
            device_id_type=MESH,
        )

    for c in range(chunks):
        for side in range(2):
            root_copy(side, 1, c).start()

    for j in range(far, ring):
        select_rows(j)

    def out_copies(slot, block):
        local = pltpu.make_async_copy(result.at[block], out_ref.at[0, block], out_local.at[slot])
        remote = pltpu.make_async_remote_copy(
            src_ref=result.at[block],
            dst_ref=out_ref.at[1, block],
            send_sem=out_send.at[slot],
            recv_sem=out_recv.at[slot],
            device_id=sibling,
            device_id_type=MESH,
        )
        return local, remote

    def out_slot(offset):
        return lax.rem(sign * offset + 4 * ring, ring)

    def send_out(offset):
        for copy in out_copies(out_slot(offset), at(offset)):
            copy.start()

    result[me] = apply_root(grad_sel[me], own_root)
    send_out(0)

    for d in range(1, reach + 1):
        for c in range(chunks):
            for side in range(2):
                root_copy(side, d, c).wait_recv()
                if d < reach:
                    root_copy(side, d + 1, c).start()
        if d < reach:
            for side in range(2):
                offset = d if side else -d
                result[at(offset)] = apply_root(grad_sel[at(offset)], roots.at[side, d - 1])
                send_out(offset)

    def back_copy(side, k):
        way = 1 if side else -1
        return pltpu.make_async_remote_copy(
            src_ref=answer.at[side, pl.ds(k * height, height)],
            dst_ref=result.at[at(way * reach)],
            send_sem=back_send.at[side, k],
            recv_sem=back_recv.at[side, k],
            device_id=to(-way * k),
            device_id_type=MESH,
        )

    def arrived(side, k):
        way = 1 if side else -1
        return pltpu.make_async_remote_copy(
            src_ref=answer.at[side, pl.ds(k * height, height)],
            dst_ref=result.at[at(way * (reach + k))],
            send_sem=back_send.at[side, k],
            recv_sem=back_recv.at[side, k],
            device_id=to(way * k),
            device_id_type=MESH,
        )

    for side in (1, 0):
        way = 1 if side else -1
        served = [k for s, k in far_sides if s == side]
        for k in served:
            row_copy(side, k).wait_recv()
        request[side, 0:height] = grad_sel[at(way * reach)]
        tall = (len(served) + 1) * height
        answer[side, 0:tall] = apply_root(request[side, 0:tall], roots.at[side, reach - 1])
        for k in reversed(served):
            back_copy(side, k).start()
        result[at(way * reach)] = answer[side, 0:height]
        send_out(way * reach)

    for side, k in sorted(far_sides, key=lambda each: each[1]):
        arrived(side, k).wait_recv()
        send_out((1 if side else -1) * (reach + k))

    for j in range(ring):
        grad_swap(j).wait_send()
    stat_swap.wait_send()
    for side, k in far_sides:
        row_copy(side, k).wait_send()
        back_copy(side, k).wait_send()
    for d in range(1, reach + 1):
        for c in range(chunks):
            for side in range(2):
                root_copy(side, d, c).wait_send()
    for offset in range(ring):
        local, remote = out_copies(offset, lax.rem(me + offset, ring))
        local.wait()
        remote.wait()


def on_device(mesh, statistics, gradients, counts):
    ring = mesh.shape["mp"]
    reach = ring // 4
    slots, blocks, height, order = gradients.shape
    half = order // 2
    chunks = 2 * half // LANES
    packed = chunks * half + TAIL
    tall = (ring // 2 - reach + 1) * height
    anywhere = pl.BlockSpec(memory_space=pl.ANY)
    dma = pltpu.SemaphoreType.DMA
    out = pl.pallas_call(
        functools.partial(kernel, ring, reach),
        out_shape=jax.ShapeDtypeStruct(gradients.shape, BF16),
        in_specs=[pl.BlockSpec(memory_space=pltpu.SMEM), anywhere, anywhere],
        out_specs=anywhere,
        scratch_shapes=[
            pltpu.VMEM((order, order), BF16),
            pltpu.VMEM((order, order), BF16),
            pltpu.VMEM((blocks, height, order), BF16),
            pltpu.VMEM((blocks, height, order), BF16),
            pltpu.VMEM((blocks, height, order), BF16),
            pltpu.VMEM((2, tall, order), BF16),
            pltpu.VMEM((2, tall, order), BF16),
            pltpu.VMEM((packed, LANES), BF16),
            pltpu.VMEM((2, reach, packed, LANES), BF16),
            pltpu.VMEM((blocks, height, order), BF16),
            dma((2,)),
            dma((ring + 1,)),
            dma((ring + 1,)),
            dma((2, ring // 2)),
            dma((2, ring // 2)),
            dma((2, reach, chunks)),
            dma((2, reach, chunks)),
            dma((2, ring // 2)),
            dma((2, ring // 2)),
            dma((ring,)),
            dma((ring,)),
            dma((ring,)),
        ],
        compiler_params=pltpu.CompilerParams(
            collective_id=0, has_side_effects=True, vmem_limit_bytes=40 * 1024 * 1024
        ),
        name="hybrid",
    )(counts, statistics, gradients)
    live = (jnp.arange(slots) < counts[0])[:, None, None, None]
    return jnp.where(live, out, jnp.zeros_like(out))


def solution(mesh):
    in_specs = (P("dp", "mp", None), P("dp", None, "mp", None), P("dp"))
    out_specs = P("dp", None, "mp", None)
    return jax.shard_map(
        functools.partial(on_device, mesh),
        mesh=mesh,
        in_specs=in_specs,
        out_specs=out_specs,
        check_vma=False,
    )
```

time: 134 us -> 66.6 us (0.50)
  the two profiles are of different devices: /device:TPU:20 before, /device:TPU:1 now
where the time goes in v2:
time: 66.6 us; the launch traced here: 66.4 us
  Pallas kernels  62.1 us (93%)
  local copies, waits for them, and re-layouts  2.44 us (4%)
  other arithmetic  1.12 us (2%)
  between operations  0.68 us (1%)
    pallas_call x1, Pallas kernels, on_device(): pl.pallas_call(functools.partial(kernel, ring, reach), out_shape=jax.Shap...  62.1 us
    unnamed x4, local copies, waits for them, and re-layouts  2.44 us

profile of v2, /device:TPU:1, one launch (start us, length us, event | category | flops | bytes accessed | tf_op | source)
XLA Modules:
  0.0 66.4 jit_solution(15493295579945043743)
XLA Ops:
  0.7 0.0 copy-start
  0.7 1.2 %copy-done = bf16[2,512,512]{2,1,0:T(8,128)(2,1)S(1)} copy-done((bf16[2,512,512]{2,1,0:T(8,128)(2,1)S(1)}, bf16[2,512,512]{2,1,0:T(8,128)(2,1)}, u32[]{:S(2)}) %copy-start) | copy-done | bytes 1048600
  1.9 0.0 copy-start.1
  1.9 1.2 %copy-done.1 = bf16[2,16,32,512]{3,2,1,0:T(8,128)(2,1)S(1)} copy-done((bf16[2,16,32,512]{3,2,1,0:T(8,128)(2,1)S(1)}, bf16[2,16,32,512]{3,2,1,0:T(8,128)(2,1)}, u32[]{:S(2)}) %copy-start.1) | copy-done | bytes 1048600
  3.1 62.1 %hybrid.1 = bf16[2,16,32,512]{3,2,1,0:T(8,128)(2,1)S(1)} custom-call(s32[1]{0:T(128)} %copy.4.counts_ref, bf16[2,512,512]{2,1,0:T(8,128)(2,1)S(1)} %copy-done, bf16[2,16,32,512]{3,2,1,0:T(8,128)(2,1)S(1)} %copy-done.1), custom_call_target="tpu_custom_call" | custom-call | tf_op jit(solution)/shard_map/hybrid/pallas_call | solution.py:324
  65.3 1.1 %broadcast_select_fusion = bf16[2,16,32,512]{3,2,1,0:T(8,128)(2,1)} fusion(bf16[2,16,32,512]{3,2,1,0:T(8,128)(2,1)S(1)} %hybrid.1, pred[2]{0:T(512)(128)(4,1)S(1)} %iota_compare_fusion), kind=kLoop, calls=%fused_computation | loop fusion | flops 524288 | bytes 2097154 | tf_op jit(solution)/shard_map/jit(_where)/select_n | solution.py:359
  (1 shorter events, 0.0 us)
Async XLA Ops:
  0.7 1.2 %copy-start = (bf16[2,512,512]{2,1,0:T(8,128)(2,1)S(1)}, bf16[2,512,512]{2,1,0:T(8,128)(2,1)}, u32[]{:S(2)}) copy-start(bf16[2,512,512]{2,1,0:T(8,128)(2,1)} %stat_ref.1) | copy-start | bytes 3145732
  1.9 1.2 %copy-start.1 = (bf16[2,16,32,512]{3,2,1,0:T(8,128)(2,1)S(1)}, bf16[2,16,32,512]{3,2,1,0:T(8,128)(2,1)}, u32[]{:S(2)}) copy-start(bf16[2,16,32,512]{3,2,1,0:T(8,128)(2,1)} %grad_ref.1) | copy-start | bytes 3145732

commit v3 on v2

v3 whole, which is shorter than its diff:
```python
import functools

import jax
import jax.numpy as jnp
from jax import lax
from jax.experimental import pallas as pl
from jax.experimental.pallas import tpu as pltpu
from jax.sharding import PartitionSpec as P

MESH = pl.DeviceIdType.MESH
LANES = 128
TAIL = 16
REACH = 4
RELAY = True
F32 = jnp.float32
BF16 = jnp.bfloat16


def dot(a, b):
    return jnp.dot(a, b, preferred_element_type=F32)


def dot_t(a, b):
    return lax.dot_general(a, b, (((1,), (1,)), ((), ())), preferred_element_type=F32)


def iotas(shape):
    return lax.broadcasted_iota(jnp.int32, shape, 0), lax.broadcasted_iota(jnp.int32, shape, 1)


def newton_root(block):
    order = block.shape[0]
    values = block.astype(F32)
    total = jnp.sum(jnp.sum(values * values, axis=1, keepdims=True), axis=0, keepdims=True)
    norm_scale = jnp.sqrt(total) + 1e-06
    scaled = (values * (1.0 / norm_scale)).astype(BF16)
    row, column = iotas((order, order))
    five = jnp.where(row == column, 5.0, 0.0).astype(F32)
    step_one = ((five - scaled.astype(F32)) * 0.25).astype(BF16)
    square = dot(step_one, step_one).astype(BF16)
    fourth = dot(square, square).astype(BF16)
    updated = dot(fourth, scaled)
    step_two = ((five - updated) * 0.25).astype(BF16)
    return dot(step_one, step_two) * lax.rsqrt(jnp.sqrt(norm_scale))


def layout(half):
    across = half * half // LANES
    corner = across // 2
    first = corner + TAIL
    return across, corner, [(0, across // 2), (across // 2, across // 2), (across, first), (across + first, corner)]


def fold(block):
    size = block.shape[0] // 2
    row, column = iotas((size, size))
    corner = block[size:, size:]
    both = jnp.where(row <= column, block[:size, :size], corner)
    diagonal = jnp.sum(jnp.where(row == column, corner, 0.0), axis=0, keepdims=True)
    return block[:size, size:].astype(BF16), both.astype(BF16), diagonal


def unfold(above, both, diagonal):
    size = both.shape[0]
    row, column = iotas((size, size))
    both = both.astype(F32)
    mirror = both.T
    first = jnp.where(row <= column, both, mirror).astype(BF16)
    last = jnp.where(row > column, both, jnp.where(row == column, diagonal, mirror)).astype(BF16)
    below = above.astype(F32).T.astype(BF16)
    return jnp.concatenate(
        [jnp.concatenate([first, above], axis=1), jnp.concatenate([below, last], axis=1)], axis=0
    )


def store_slabs(ref, start, block):
    height, width = block.shape
    for j in range(width // LANES):
        ref[start + j * height : start + (j + 1) * height, :] = block[:, j * LANES : (j + 1) * LANES]
    return start + height * width // LANES


def load_slabs(ref, start, height, width):
    slabs = [ref[start + j * height : start + (j + 1) * height, :] for j in range(width // LANES)]
    return jnp.concatenate(slabs, axis=1) if len(slabs) > 1 else slabs[0]


def pack(root, ref):
    half = root.shape[0] // 2
    size = half // 2
    across, corner, _ = layout(half)
    store_slabs(ref, 0, root[:half, half:].astype(BF16))
    above_0, both_0, diagonal_0 = fold(root[:half, :half])
    above_1, both_1, diagonal_1 = fold(root[half:, half:])
    end = store_slabs(ref, store_slabs(ref, across, above_0), both_0)
    tail_row, _ = iotas((TAIL, size))
    tail = jnp.where(tail_row == 0, diagonal_0, jnp.where(tail_row == 1, diagonal_1, 0.0))
    ref[end : end + TAIL, :] = tail.astype(BF16)
    store_slabs(ref, store_slabs(ref, end + TAIL, above_1), both_1)


def unpack_across(ref, half):
    return load_slabs(ref, 0, half, half)


def unpack_corner(ref, half, which):
    across, corner, _ = layout(half)
    size = half // 2
    start = across + which * (corner + TAIL)
    above = load_slabs(ref, start, size, size)
    both = load_slabs(ref, start + corner // 2, size, size)
    tail = ref[across + corner : across + corner + TAIL, :].astype(F32)
    return unfold(above, both, tail[which : which + 1, :])


def left_half(rows, ref):
    half = rows.shape[1] // 2
    left, right = rows[:, :half], rows[:, half:]
    return (dot(left, unpack_corner(ref, half, 0)) + dot_t(right, unpack_across(ref, half))).astype(BF16)


def right_half(rows, ref):
    half = rows.shape[1] // 2
    left, right = rows[:, :half], rows[:, half:]
    return (dot(left, unpack_across(ref, half)) + dot(right, unpack_corner(ref, half, 1))).astype(BF16)


def apply_root(rows, ref):
    return jnp.concatenate([left_half(rows, ref), right_half(rows, ref)], axis=1)


def kernel(
    ring,
    reach,
    counts_ref,
    stat_ref,
    grad_ref,
    out_ref,
    stat_own,
    stat_sib,
    grad_own,
    grad_sib,
    grad_sel,
    request,
    answer,
    own_root,
    roots,
    result,
    local_sem,
    sib_send,
    sib_recv,
    row_send,
    row_recv,
    root_send,
    root_recv,
    back_send,
    back_recv,
    out_local,
    out_send,
    out_recv,
    ready,
):
    dp, me = lax.axis_index("dp"), lax.axis_index("mp")
    core = lax.rem(dp, 2)
    sibling = {"dp": dp + 1 - 2 * core}
    sign = 1 - 2 * core
    order = stat_own.shape[0]
    half = order // 2
    pieces = layout(half)[2]
    chunks = len(pieces)
    height = grad_own.shape[1]

    def at(offset):
        return lax.rem(me + sign * offset + 4 * ring, ring)

    def to(offset):
        return {"mp": at(offset)}

    stat_copy = pltpu.make_async_copy(stat_ref.at[0], stat_own, local_sem.at[0])
    grad_copy = pltpu.make_async_copy(grad_ref.at[0], grad_own, local_sem.at[1])
    grad_copy.start()
    stat_copy.start()

    barrier = pltpu.get_barrier_semaphore()
    pl.semaphore_signal(barrier, inc=1, device_id=sibling, device_id_type=MESH)
    span = max(1, ring // 2 - reach)
    direct = 1 if RELAY else span
    for d in range(1, direct + 1):
        pl.semaphore_signal(barrier, inc=1, device_id=to(d), device_id_type=MESH)
        pl.semaphore_signal(barrier, inc=1, device_id=to(-d), device_id_type=MESH)
    pl.semaphore_wait(barrier, 2 * direct + 1)

    def tell(d):
        if RELAY and d <= span:
            pl.semaphore_signal(ready.at[0, d], inc=1, device_id=to(1), device_id_type=MESH)
            pl.semaphore_signal(ready.at[1, d], inc=1, device_id=to(-1), device_id_type=MESH)

    def heard(d):
        if RELAY and 1 < d <= span:
            pl.semaphore_wait(ready.at[0, d], 1)
            pl.semaphore_wait(ready.at[1, d], 1)
            tell(d + 1)

    tell(2)

    def grad_swap(block):
        j = lax.rem(block - me + ring, ring)
        return pltpu.make_async_remote_copy(
            src_ref=grad_ref.at[1, block],
            dst_ref=grad_sib.at[block],
            send_sem=sib_send.at[j],
            recv_sem=sib_recv.at[j],
            device_id=sibling,
            device_id_type=MESH,
        )

    stat_swap = pltpu.make_async_remote_copy(
        src_ref=stat_ref.at[1],
        dst_ref=stat_sib,
        send_sem=sib_send.at[ring],
        recv_sem=sib_recv.at[ring],
        device_id=sibling,
        device_id_type=MESH,
    )
    far_sides = [(1, ring // 2 - reach)]
    for k in range(ring // 2 - reach - 1, 0, -1):
        far_sides += [(1, k), (0, k)]
    nearest_first = far_sides[::-1]
    row_order = nearest_first if RELAY else far_sides

    def far_block(side, k):
        return at((1 if side else -1) * (reach + k))

    for side, k in row_order:
        grad_swap(far_block(side, k)).start()
    stat_swap.start()
    for d in range(-reach, reach + 1):
        grad_swap(at(d)).start()

    own_first = counts_ref[0] >= 1

    def select_rows(block):
        grad_swap(block).wait_recv()
        grad_sel[block] = jnp.where(own_first, grad_own[block], grad_sib[block])

    def row_copy(side, k):
        way = 1 if side else -1
        return pltpu.make_async_remote_copy(
            src_ref=grad_sel.at[far_block(side, k)],
            dst_ref=request.at[side, pl.ds(k * height, height)],
            send_sem=row_send.at[side, k],
            recv_sem=row_recv.at[side, k],
            device_id=to(way * k),
            device_id_type=MESH,
        )

    grad_copy.wait()
    heard(2)
    last = 2
    for side, k in row_order:
        select_rows(far_block(side, k))
        while last < k:
            last += 1
            heard(last)
        row_copy(side, k).start()

    stat_copy.wait()
    stat_swap.wait_recv()
    pack(newton_root(jnp.where(own_first, stat_own[...], stat_sib[...])), own_root)

    def piece(c):
        return pl.ds(*pieces[c])

    def root_copy(side, d, c):
        source = own_root if d == 1 else roots.at[side, d - 2]
        return pltpu.make_async_remote_copy(
            src_ref=source.at[piece(c)],
            dst_ref=roots.at[side, d - 1, piece(c)],
            send_sem=root_send.at[side, d - 1, c],
            recv_sem=root_recv.at[side, d - 1, c],
            device_id=to(-1 if side else 1),
            device_id_type=MESH,
        )

    for c in range(chunks):
        for side in range(2):
            root_copy(side, 1, c).start()

    for d in range(-reach, reach + 1):
        select_rows(at(d))

    def columns(part):
        return pl.ds(part * half, half)

    def out_copies(slot, block, part):
        place = (block, slice(None), columns(part))
        local = pltpu.make_async_copy(
            result.at[place], out_ref.at[(0, *place)], out_local.at[part, slot]
        )
        remote = pltpu.make_async_remote_copy(
            src_ref=result.at[place],
            dst_ref=out_ref.at[(1, *place)],
            send_sem=out_send.at[part, slot],
            recv_sem=out_recv.at[part, slot],
            device_id=sibling,
            device_id_type=MESH,
        )
        return local, remote

    def out_slot(offset):
        return lax.rem(sign * offset + 4 * ring, ring)

    def send_out(offset, parts=(0, 1)):
        for part in parts:
            for copy in out_copies(out_slot(offset), at(offset), part):
                copy.start()

    result[me] = apply_root(grad_sel[me], own_root)
    send_out(0)

    for d in range(1, reach):
        for c in range(chunks):
            for side in range(2):
                root_copy(side, d, c).wait_recv()
                root_copy(side, d + 1, c).start()
        for side in range(2):
            offset = d if side else -d
            result[at(offset)] = apply_root(grad_sel[at(offset)], roots.at[side, d - 1])
            send_out(offset)

    def back_copy(side, k, part):
        way = 1 if side else -1
        return pltpu.make_async_remote_copy(
            src_ref=answer.at[side, part, pl.ds(k * height, height)],
            dst_ref=result.at[at(way * reach), :, columns(part)],
            send_sem=back_send.at[side, part, k],
            recv_sem=back_recv.at[side, part, k],
            device_id=to(-way * k),
            device_id_type=MESH,
        )

    def arrived(side, k, part):
        way = 1 if side else -1
        return pltpu.make_async_remote_copy(
            src_ref=answer.at[side, part, pl.ds(k * height, height)],
            dst_ref=result.at[at(way * (reach + k)), :, columns(part)],
            send_sem=back_send.at[side, part, k],
            recv_sem=back_recv.at[side, part, k],
            device_id=to(way * k),
            device_id_type=MESH,
        )

    served = [[k for s, k in far_sides if s == side] for side in range(2)]
    for side in (1, 0):
        for k in served[side]:
            row_copy(side, k).wait_recv()
        request[side, 0:height] = grad_sel[at((1 if side else -1) * reach)]
    for part, needed in ((0, range(chunks - 1)), (1, (chunks - 1,))):
        for side in (1, 0):
            offset = reach if side else -reach
            tall = (len(served[side]) + 1) * height
            for c in needed:
                root_copy(side, reach, c).wait_recv()
            product = (right_half if part else left_half)(request[side, 0:tall], roots.at[side, reach - 1])
            answer[side, part, 0:tall] = product
            for k in served[side]:
                back_copy(side, k, part).start()
            result[at(offset), :, part * half : (part + 1) * half] = product[0:height]
            send_out(offset, (part,))

    for part in range(2):
        for side, k in reversed(far_sides):
            arrived(side, k, part).wait_recv()
            send_out((1 if side else -1) * (reach + k), (part,))

    for offset in range(ring):
        grad_swap(lax.rem(me + offset, ring)).wait_send()
    stat_swap.wait_send()
    for side, k in far_sides:
        row_copy(side, k).wait_send()
        for part in range(2):
            back_copy(side, k, part).wait_send()
    for d in range(1, reach + 1):
        for c in range(chunks):
            for side in range(2):
                root_copy(side, d, c).wait_send()
    for offset in range(ring):
        for part in range(2):
            local, remote = out_copies(offset, lax.rem(me + offset, ring), part)
            local.wait()
            remote.wait()


def on_device(mesh, statistics, gradients, counts):
    ring = mesh.shape["mp"]
    reach = REACH
    slots, blocks, height, order = gradients.shape
    half = order // 2
    pieces = layout(half)[2]
    chunks, packed = len(pieces), sum(pieces[-1])
    tall = (ring // 2 - reach + 1) * height
    anywhere = pl.BlockSpec(memory_space=pl.ANY)
    in_hbm = pl.BlockSpec(memory_space=pltpu.HBM)
    dma = pltpu.SemaphoreType.DMA
    out = pl.pallas_call(
        functools.partial(kernel, ring, reach),
        out_shape=jax.ShapeDtypeStruct(gradients.shape, BF16),
        in_specs=[pl.BlockSpec(memory_space=pltpu.SMEM), in_hbm, in_hbm],
        out_specs=anywhere,
        scratch_shapes=[
            pltpu.VMEM((order, order), BF16),
            pltpu.VMEM((order, order), BF16),
            pltpu.VMEM((blocks, height, order), BF16),
            pltpu.VMEM((blocks, height, order), BF16),
            pltpu.VMEM((blocks, height, order), BF16),
            pltpu.VMEM((2, tall, order), BF16),
            pltpu.VMEM((2, 2, tall, half), BF16),
            pltpu.VMEM((packed, LANES), BF16),
            pltpu.VMEM((2, reach, packed, LANES), BF16),
            pltpu.VMEM((blocks, height, order), BF16),
            dma((2,)),
            dma((ring + 1,)),
            dma((ring + 1,)),
            dma((2, ring // 2)),
            dma((2, ring // 2)),
            dma((2, reach, chunks)),
            dma((2, reach, chunks)),
            dma((2, 2, ring // 2)),
            dma((2, 2, ring // 2)),
            dma((2, ring)),
            dma((2, ring)),
            dma((2, ring)),
            pltpu.SemaphoreType.REGULAR((2, ring // 2)),
        ],
        compiler_params=pltpu.CompilerParams(
            collective_id=0, has_side_effects=True, vmem_limit_bytes=52 * 1024 * 1024
        ),
        name="hybrid",
    )(counts, statistics, gradients)
    live = (jnp.arange(slots) < counts[0])[:, None, None, None]
    return jnp.where(live, out, jnp.zeros_like(out))


def solution(mesh):
    in_specs = (P("dp", "mp", None), P("dp", None, "mp", None), P("dp"))
    out_specs = P("dp", None, "mp", None)
    return jax.shard_map(
        functools.partial(on_device, mesh),
        mesh=mesh,
        in_specs=in_specs,
        out_specs=out_specs,
        check_vma=False,
    )
```

time: 66.6 us -> 61.9 us (0.929)
  local copies, waits for them, and re-layouts: 2.44 us -> 0 us
  Pallas kernels: 62.1 us -> 59.9 us
    unnamed x4 -> x0, local copies, waits for them, and re-layouts: 2.44 us -> none
    pallas_call x1, Pallas kernels: 62.1 us -> 59.9 us  [on_device(): pl.pallas_call(functools.partial(kernel, ring, reach), out_shape=jax.Shap...]
where the time goes in v3:
time: 61.9 us; the launch traced here: 61.7 us
  Pallas kernels  59.9 us (97%)
  other arithmetic  1.12 us (2%)
  between operations  0.67 us (1%)
    pallas_call x1, Pallas kernels, on_device(): pl.pallas_call(functools.partial(kernel, ring, reach), out_shape=jax.Shap...  59.9 us

profile of v3, /device:TPU:1, one launch (start us, length us, event | category | flops | bytes accessed | tf_op | source)
XLA Modules:
  0.0 61.7 jit_solution(6413783349921413133)
XLA Ops:
  0.7 59.9 %hybrid.1 = bf16[2,16,32,512]{3,2,1,0:T(8,128)(2,1)S(1)} custom-call(s32[1]{0:T(128)} %copy.4.counts_ref, bf16[2,512,512]{2,1,0:T(8,128)(2,1)} %stat_ref.1, bf16[2,16,32,512]{3,2,1,0:T(8,128)(2,1)} %grad_ref.1), custom_call_target="tpu_custom_call" | custom-call | tf_op jit(solution)/shard_map/hybrid/pallas_call | solution.py:405
  60.6 1.1 %broadcast_select_fusion = bf16[2,16,32,512]{3,2,1,0:T(8,128)(2,1)} fusion(bf16[2,16,32,512]{3,2,1,0:T(8,128)(2,1)S(1)} %hybrid.1, pred[2]{0:T(512)(128)(4,1)S(1)} %iota_compare_fusion), kind=kLoop, calls=%fused_computation | loop fusion | flops 524288 | bytes 2097154 | tf_op jit(solution)/shard_map/jit(_where)/select_n | solution.py:441
  (1 shorter events, 0.0 us)

commit v4 on v3

--- a/solution.py
+++ b/solution.py
@@ -45,10 +45,9 @@
 
 
 def layout(half):
-    across = half * half // LANES
-    corner = across // 2
-    first = corner + TAIL
-    return across, corner, [(0, across // 2), (across // 2, across // 2), (across, first), (across + first, corner)]
+    size = half * half // 2 // LANES
+    lengths = [size, size + TAIL, size, size]
+    return [(sum(lengths[:n]), lengths[n]) for n in range(len(lengths))]
 
 
 def fold(block):
@@ -88,45 +87,51 @@
 def pack(root, ref):
     half = root.shape[0] // 2
     size = half // 2
-    across, corner, _ = layout(half)
-    store_slabs(ref, 0, root[:half, half:].astype(BF16))
+    starts = [start for start, _ in layout(half)]
+    across = root[:half, half:].astype(BF16)
     above_0, both_0, diagonal_0 = fold(root[:half, :half])
     above_1, both_1, diagonal_1 = fold(root[half:, half:])
-    end = store_slabs(ref, store_slabs(ref, across, above_0), both_0)
+    store_slabs(ref, starts[0], across[:size])
+    end = store_slabs(ref, store_slabs(ref, starts[1], above_0), both_0)
     tail_row, _ = iotas((TAIL, size))
     tail = jnp.where(tail_row == 0, diagonal_0, jnp.where(tail_row == 1, diagonal_1, 0.0))
     ref[end : end + TAIL, :] = tail.astype(BF16)
-    store_slabs(ref, store_slabs(ref, end + TAIL, above_1), both_1)
-
-
-def unpack_across(ref, half):
-    return load_slabs(ref, 0, half, half)
+    store_slabs(ref, starts[2], across[size:])
+    store_slabs(ref, store_slabs(ref, starts[3], above_1), both_1)
+
+
+def unpack_across(ref, half, which):
+    return load_slabs(ref, layout(half)[2 * which][0], half // 2, half)
 
 
 def unpack_corner(ref, half, which):
-    across, corner, _ = layout(half)
     size = half // 2
-    start = across + which * (corner + TAIL)
+    starts = [start for start, _ in layout(half)]
+    start = starts[1 + 2 * which]
     above = load_slabs(ref, start, size, size)
-    both = load_slabs(ref, start + corner // 2, size, size)
-    tail = ref[across + corner : across + corner + TAIL, :].astype(F32)
+    both = load_slabs(ref, start + size * size // LANES, size, size)
+    tail = ref[starts[2] - TAIL : starts[2], :].astype(F32)
     return unfold(above, both, tail[which : which + 1, :])
 
 
-def left_half(rows, ref):
+def apply_part(rows, ref, part):
+    half = rows.shape[1] // 2
+    size = half // 2
+    left, right = rows[:, :half], rows[:, half:]
+    if part < 2:
+        corner = unpack_corner(ref, half, 0)[:, part * size : (part + 1) * size]
+        return (dot(left, corner) + dot_t(right, unpack_across(ref, half, part))).astype(BF16)
+    across = jnp.concatenate([unpack_across(ref, half, 0), unpack_across(ref, half, 1)], axis=0)
+    return (dot(left, across) + dot(right, unpack_corner(ref, half, 1))).astype(BF16)
+
+
+def apply_root(rows, ref):
     half = rows.shape[1] // 2
     left, right = rows[:, :half], rows[:, half:]
-    return (dot(left, unpack_corner(ref, half, 0)) + dot_t(right, unpack_across(ref, half))).astype(BF16)
-
-
-def right_half(rows, ref):
-    half = rows.shape[1] // 2
-    left, right = rows[:, :half], rows[:, half:]
-    return (dot(left, unpack_across(ref, half)) + dot(right, unpack_corner(ref, half, 1))).astype(BF16)
-
-
-def apply_root(rows, ref):
-    return jnp.concatenate([left_half(rows, ref), right_half(rows, ref)], axis=1)
+    across = jnp.concatenate([unpack_across(ref, half, 0), unpack_across(ref, half, 1)], axis=0)
+    out_left = dot(left, unpack_corner(ref, half, 0)) + dot_t(right, across)
+    out_right = dot(left, across) + dot(right, unpack_corner(ref, half, 1))
+    return jnp.concatenate([out_left, out_right], axis=1).astype(BF16)
 
 
 def kernel(
@@ -155,9 +160,7 @@
     root_recv,
     back_send,
     back_recv,
-    out_local,
-    out_send,
-    out_recv,
+    out_sem,
     ready,
 ):
     dp, me = lax.axis_index("dp"), lax.axis_index("mp")
@@ -166,8 +169,9 @@
     sign = 1 - 2 * core
     order = stat_own.shape[0]
     half = order // 2
-    pieces = layout(half)[2]
+    pieces = layout(half)
     chunks = len(pieces)
+    parts = [(0, half // 2), (half // 2, half // 2), (half, half)]
     height = grad_own.shape[1]
 
     def at(offset):
@@ -208,7 +212,7 @@
         return pltpu.make_async_remote_copy(
             src_ref=grad_ref.at[1, block],
             dst_ref=grad_sib.at[block],
-            send_sem=sib_send.at[j],
+            send_sem=sib_send.at[0],
             recv_sem=sib_recv.at[j],
             device_id=sibling,
             device_id_type=MESH,
@@ -217,7 +221,7 @@
     stat_swap = pltpu.make_async_remote_copy(
         src_ref=stat_ref.at[1],
         dst_ref=stat_sib,
-        send_sem=sib_send.at[ring],
+        send_sem=sib_send.at[1],
         recv_sem=sib_recv.at[ring],
         device_id=sibling,
         device_id_type=MESH,
@@ -248,7 +252,7 @@
         return pltpu.make_async_remote_copy(
             src_ref=grad_sel.at[far_block(side, k)],
             dst_ref=request.at[side, pl.ds(k * height, height)],
-            send_sem=row_send.at[side, k],
+            send_sem=row_send.at[0],
             recv_sem=row_recv.at[side, k],
             device_id=to(way * k),
             device_id_type=MESH,
@@ -276,7 +280,7 @@
         return pltpu.make_async_remote_copy(
             src_ref=source.at[piece(c)],
             dst_ref=roots.at[side, d - 1, piece(c)],
-            send_sem=root_send.at[side, d - 1, c],
+            send_sem=root_send.at[0],
             recv_sem=root_recv.at[side, d - 1, c],
             device_id=to(-1 if side else 1),
             device_id_type=MESH,
@@ -289,31 +293,22 @@
     for d in range(-reach, reach + 1):
         select_rows(at(d))
 
-    def columns(part):
-        return pl.ds(part * half, half)
-
-    def out_copies(slot, block, part):
-        place = (block, slice(None), columns(part))
-        local = pltpu.make_async_copy(
-            result.at[place], out_ref.at[(0, *place)], out_local.at[part, slot]
-        )
+    def out_copies(source, own, other):
+        local = pltpu.make_async_copy(source, own, out_sem.at[0])
         remote = pltpu.make_async_remote_copy(
-            src_ref=result.at[place],
-            dst_ref=out_ref.at[(1, *place)],
-            send_sem=out_send.at[part, slot],
-            recv_sem=out_recv.at[part, slot],
+            src_ref=source,
+            dst_ref=other,
+            send_sem=out_sem.at[1],
+            recv_sem=out_sem.at[2],
             device_id=sibling,
             device_id_type=MESH,
         )
         return local, remote
 
-    def out_slot(offset):
-        return lax.rem(sign * offset + 4 * ring, ring)
-
-    def send_out(offset, parts=(0, 1)):
-        for part in parts:
-            for copy in out_copies(out_slot(offset), at(offset), part):
-                copy.start()
+    def send_out(offset, start=0, width=order):
+        place = (at(offset), slice(None), pl.ds(start, width))
+        for copy in out_copies(result.at[place], out_ref.at[(0, *place)], out_ref.at[(1, *place)]):
+            copy.start()
 
     result[me] = apply_root(grad_sel[me], own_root)
     send_out(0)
@@ -331,9 +326,9 @@
     def back_copy(side, k, part):
         way = 1 if side else -1
         return pltpu.make_async_remote_copy(
-            src_ref=answer.at[side, part, pl.ds(k * height, height)],
-            dst_ref=result.at[at(way * reach), :, columns(part)],
-            send_sem=back_send.at[side, part, k],
+            src_ref=answer.at[side, pl.ds(k * height, height), pl.ds(*parts[part])],
+            dst_ref=result.at[at(way * reach), :, pl.ds(*parts[part])],
+            send_sem=back_send.at[0],
             recv_sem=back_recv.at[side, part, k],
             device_id=to(-way * k),
             device_id_type=MESH,
@@ -342,9 +337,9 @@
     def arrived(side, k, part):
         way = 1 if side else -1
         return pltpu.make_async_remote_copy(
-            src_ref=answer.at[side, part, pl.ds(k * height, height)],
-            dst_ref=result.at[at(way * (reach + k)), :, columns(part)],
-            send_sem=back_send.at[side, part, k],
+            src_ref=answer.at[side, pl.ds(k * height, height), pl.ds(*parts[part])],
+            dst_ref=result.at[at(way * (reach + k)), :, pl.ds(*parts[part])],
+            send_sem=back_send.at[0],
             recv_sem=back_recv.at[side, part, k],
             device_id=to(way * k),
             device_id_type=MESH,
@@ -354,41 +349,46 @@
     for side in (1, 0):
         for k in served[side]:
             row_copy(side, k).wait_recv()
-        request[side, 0:height] = grad_sel[at((1 if side else -1) * reach)]
-    for part, needed in ((0, range(chunks - 1)), (1, (chunks - 1,))):
+    for part, needed in ((0, (0, 1)), (1, (2,)), (2, (3,))):
         for side in (1, 0):
-            offset = reach if side else -reach
-            tall = (len(served[side]) + 1) * height
+            rows = slice(height, (len(served[side]) + 1) * height)
+            start, width = parts[part]
             for c in needed:
                 root_copy(side, reach, c).wait_recv()
-            product = (right_half if part else left_half)(request[side, 0:tall], roots.at[side, reach - 1])
-            answer[side, part, 0:tall] = product
+            answer[side, rows, start : start + width] = apply_part(
+                request[side, rows], roots.at[side, reach - 1], part
+            )
             for k in served[side]:
                 back_copy(side, k, part).start()
-            result[at(offset), :, part * half : (part + 1) * half] = product[0:height]
-            send_out(offset, (part,))
-
-    for part in range(2):
-        for side, k in reversed(far_sides):
+    for side in (1, 0):
+        offset = reach if side else -reach
+        result[at(offset)] = apply_root(grad_sel[at(offset)], roots.at[side, reach - 1])
+        send_out(offset)
+
+    def all_sent(source, sem):
+        pltpu.make_async_remote_copy(
+            src_ref=source,
+            dst_ref=source,
+            send_sem=sem,
+            recv_sem=sib_recv.at[0],
+            device_id=sibling,
+            device_id_type=MESH,
+        ).wait_send()
+
+    all_sent(grad_sib, sib_send.at[0])
+    all_sent(stat_sib, sib_send.at[1])
+    all_sent(grad_sel.at[pl.ds(0, len(far_sides))], row_send.at[0])
+    all_sent(roots, root_send.at[0])
+
+    for part in range(3):
+        for side, k in far_sides:
             arrived(side, k, part).wait_recv()
-            send_out((1 if side else -1) * (reach + k), (part,))
-
-    for offset in range(ring):
-        grad_swap(lax.rem(me + offset, ring)).wait_send()
-    stat_swap.wait_send()
-    for side, k in far_sides:
-        row_copy(side, k).wait_send()
-        for part in range(2):
-            back_copy(side, k, part).wait_send()
-    for d in range(1, reach + 1):
-        for c in range(chunks):
-            for side in range(2):
-                root_copy(side, d, c).wait_send()
-    for offset in range(ring):
-        for part in range(2):
-            local, remote = out_copies(offset, lax.rem(me + offset, ring), part)
-            local.wait()
-            remote.wait()
+            if part > 0:
+                send_out((1 if side else -1) * (reach + k), (part - 1) * half, half)
+
+    all_sent(grad_sel.at[pl.ds(0, len(far_sides))], back_send.at[0])
+    for copy in out_copies(result, out_ref.at[0], out_ref.at[1]):
+        copy.wait()
 
 
 def on_device(mesh, statistics, gradients, counts):
@@ -396,7 +396,7 @@
     reach = REACH
     slots, blocks, height, order = gradients.shape
     half = order // 2
-    pieces = layout(half)[2]
+    pieces = layout(half)
     chunks, packed = len(pieces), sum(pieces[-1])
     tall = (ring // 2 - reach + 1) * height
     anywhere = pl.BlockSpec(memory_space=pl.ANY)
@@ -414,22 +414,20 @@
             pltpu.VMEM((blocks, height, order), BF16),
             pltpu.VMEM((blocks, height, order), BF16),
             pltpu.VMEM((2, tall, order), BF16),
-            pltpu.VMEM((2, 2, tall, half), BF16),
+            pltpu.VMEM((2, tall, order), BF16),
             pltpu.VMEM((packed, LANES), BF16),
             pltpu.VMEM((2, reach, packed, LANES), BF16),
             pltpu.VMEM((blocks, height, order), BF16),
             dma((2,)),
+            dma((2,)),
             dma((ring + 1,)),
-            dma((ring + 1,)),
+            dma((1,)),
             dma((2, ring // 2)),
-            dma((2, ring // 2)),
+            dma((1,)),
             dma((2, reach, chunks)),
-            dma((2, reach, chunks)),
-            dma((2, 2, ring // 2)),
-            dma((2, 2, ring // 2)),
-            dma((2, ring)),
-            dma((2, ring)),
-            dma((2, ring)),
+            dma((1,)),
+            dma((2, 3, ring // 2)),
+            dma((3,)),
             pltpu.SemaphoreType.REGULAR((2, ring // 2)),
         ],
         compiler_params=pltpu.CompilerParams(

time: 61.9 us -> 60.2 us (0.973)
  Pallas kernels: 59.9 us -> 58.2 us
    pallas_call x1, Pallas kernels: 59.9 us -> 58.2 us  [on_device(): pl.pallas_call(functools.partial(kernel, ring, reach), out_shape=jax.Shap...]
where the time goes in v4:
time: 60.2 us; the launch traced here: 60 us
  Pallas kernels  58.2 us (97%)
  other arithmetic  1.12 us (2%)
  between operations  0.67 us (1%)
    pallas_call x1, Pallas kernels, on_device(): pl.pallas_call(functools.partial(kernel, ring, reach), out_shape=jax.Shap...  58.2 us

profile of v4, /device:TPU:1, one launch (start us, length us, event | category | flops | bytes accessed | tf_op | source)
XLA Modules:
  0.0 60.0 jit_solution(2762622157334963647)
XLA Ops:
  0.7 58.2 %hybrid.1 = bf16[2,16,32,512]{3,2,1,0:T(8,128)(2,1)S(1)} custom-call(s32[1]{0:T(128)} %copy.4.counts_ref, bf16[2,512,512]{2,1,0:T(8,128)(2,1)} %stat_ref.1, bf16[2,16,32,512]{3,2,1,0:T(8,128)(2,1)} %grad_ref.1), custom_call_target="tpu_custom_call" | custom-call | tf_op jit(solution)/shard_map/hybrid/pallas_call | solution.py:405
  58.9 1.1 %broadcast_select_fusion = bf16[2,16,32,512]{3,2,1,0:T(8,128)(2,1)} fusion(bf16[2,16,32,512]{3,2,1,0:T(8,128)(2,1)S(1)} %hybrid.1, pred[2]{0:T(512)(128)(4,1)S(1)} %iota_compare_fusion), kind=kLoop, calls=%fused_computation | loop fusion | flops 524288 | bytes 2097154 | tf_op jit(solution)/shard_map/jit(_where)/select_n | solution.py:439
  (1 shorter events, 0.0 us)

commit v5 on v4

--- a/solution.py
+++ b/solution.py
@@ -207,8 +207,8 @@
 
     tell(2)
 
-    def grad_swap(block):
-        j = lax.rem(block - me + ring, ring)
+    def grad_swap(block, near=False):
+        j = 0 if near else lax.rem(block - me + ring, ring)
         return pltpu.make_async_remote_copy(
             src_ref=grad_ref.at[1, block],
             dst_ref=grad_sib.at[block],
@@ -222,7 +222,7 @@
         src_ref=stat_ref.at[1],
         dst_ref=stat_sib,
         send_sem=sib_send.at[1],
-        recv_sem=sib_recv.at[ring],
+        recv_sem=sib_recv.at[1],
         device_id=sibling,
         device_id_type=MESH,
     )
@@ -239,12 +239,11 @@
         grad_swap(far_block(side, k)).start()
     stat_swap.start()
     for d in range(-reach, reach + 1):
-        grad_swap(at(d)).start()
+        grad_swap(at(d), near=True).start()
 
     own_first = counts_ref[0] >= 1
 
     def select_rows(block):
-        grad_swap(block).wait_recv()
         grad_sel[block] = jnp.where(own_first, grad_own[block], grad_sib[block])
 
     def row_copy(side, k):
@@ -253,7 +252,7 @@
             src_ref=grad_sel.at[far_block(side, k)],
             dst_ref=request.at[side, pl.ds(k * height, height)],
             send_sem=row_send.at[0],
-            recv_sem=row_recv.at[side, k],
+            recv_sem=row_recv.at[0],
             device_id=to(way * k),
             device_id_type=MESH,
         )
@@ -262,6 +261,7 @@
     heard(2)
     last = 2
     for side, k in row_order:
+        grad_swap(far_block(side, k)).wait_recv()
         select_rows(far_block(side, k))
         while last < k:
             last += 1
@@ -290,6 +290,17 @@
         for side in range(2):
             root_copy(side, 1, c).start()
 
+    def all_here(place, sem):
+        pltpu.make_async_remote_copy(
+            src_ref=place,
+            dst_ref=place,
+            send_sem=sib_send.at[0],
+            recv_sem=sem,
+            device_id=sibling,
+            device_id_type=MESH,
+        ).wait_recv()
+
+    all_here(grad_sib.at[pl.ds(0, 2 * reach + 1)], sib_recv.at[0])
     for d in range(-reach, reach + 1):
         select_rows(at(d))
 
@@ -329,7 +340,7 @@
             src_ref=answer.at[side, pl.ds(k * height, height), pl.ds(*parts[part])],
             dst_ref=result.at[at(way * reach), :, pl.ds(*parts[part])],
             send_sem=back_send.at[0],
-            recv_sem=back_recv.at[side, part, k],
+            recv_sem=back_recv.at[side, k if part == 2 else 0],
             device_id=to(-way * k),
             device_id_type=MESH,
         )
@@ -340,15 +351,13 @@
             src_ref=answer.at[side, pl.ds(k * height, height), pl.ds(*parts[part])],
             dst_ref=result.at[at(way * (reach + k)), :, pl.ds(*parts[part])],
             send_sem=back_send.at[0],
-            recv_sem=back_recv.at[side, part, k],
+            recv_sem=back_recv.at[side, k if part == 2 else 0],
             device_id=to(way * k),
             device_id_type=MESH,
         )
 
     served = [[k for s, k in far_sides if s == side] for side in range(2)]
-    for side in (1, 0):
-        for k in served[side]:
-            row_copy(side, k).wait_recv()
+    all_here(grad_sel.at[pl.ds(0, len(far_sides))], row_recv.at[0])
     for part, needed in ((0, (0, 1)), (1, (2,)), (2, (3,))):
         for side in (1, 0):
             rows = slice(height, (len(served[side]) + 1) * height)
@@ -380,12 +389,13 @@
     all_sent(grad_sel.at[pl.ds(0, len(far_sides))], row_send.at[0])
     all_sent(roots, root_send.at[0])
 
-    for part in range(3):
-        for side, k in far_sides:
-            arrived(side, k, part).wait_recv()
-            if part > 0:
-                send_out((1 if side else -1) * (reach + k), (part - 1) * half, half)
-
+    for side in range(2):
+        all_here(answer.at[side, pl.ds(0, len(served[side]) * height), pl.ds(0, half)], back_recv.at[side, 0])
+    for side, k in far_sides:
+        send_out((1 if side else -1) * (reach + k), 0, half)
+    for side, k in far_sides:
+        arrived(side, k, 2).wait_recv()
+        send_out((1 if side else -1) * (reach + k), half, half)
     all_sent(grad_sel.at[pl.ds(0, len(far_sides))], back_send.at[0])
     for copy in out_copies(result, out_ref.at[0], out_ref.at[1]):
         copy.wait()
@@ -420,15 +430,15 @@
             pltpu.VMEM((blocks, height, order), BF16),
             dma((2,)),
             dma((2,)),
-            dma((ring + 1,)),
+            dma((ring - reach,)),
             dma((1,)),
-            dma((2, ring // 2)),
+            dma((1,)),
             dma((1,)),
             dma((2, reach, chunks)),
             dma((1,)),
-            dma((2, 3, ring // 2)),
+            dma((2, ring // 2 - reach + 1)),
             dma((3,)),
-            pltpu.SemaphoreType.REGULAR((2, ring // 2)),
+            pltpu.SemaphoreType.REGULAR((2, ring // 2 - reach + 1)),
         ],
         compiler_params=pltpu.CompilerParams(
             collective_id=0, has_side_effects=True, vmem_limit_bytes=52 * 1024 * 1024

time: 60.2 us -> 59.6 us (0.990)
  no operation moved by 1% of the time
where the time goes in v5:
time: 59.6 us; the launch traced here: 59.4 us
  Pallas kernels  57.7 us (97%)
  other arithmetic  1.12 us (2%)
  between operations  0.67 us (1%)
    pallas_call x1, Pallas kernels, on_device(): pl.pallas_call(functools.partial(kernel, ring, reach), out_shape=jax.Shap...  57.7 us

profile of v5, /device:TPU:1, one launch (start us, length us, event | category | flops | bytes accessed | tf_op | source)
XLA Modules:
  0.0 59.4 jit_solution(5598824540332485320)
XLA Ops:
  0.7 57.7 %hybrid.1 = bf16[2,16,32,512]{3,2,1,0:T(8,128)(2,1)S(1)} custom-call(s32[1]{0:T(128)} %copy.4.counts_ref, bf16[2,512,512]{2,1,0:T(8,128)(2,1)} %stat_ref.1, bf16[2,16,32,512]{3,2,1,0:T(8,128)(2,1)} %grad_ref.1), custom_call_target="tpu_custom_call" | custom-call | tf_op jit(solution)/shard_map/hybrid/pallas_call | solution.py:415
  58.3 1.1 %broadcast_select_fusion = bf16[2,16,32,512]{3,2,1,0:T(8,128)(2,1)} fusion(bf16[2,16,32,512]{3,2,1,0:T(8,128)(2,1)S(1)} %hybrid.1, pred[2]{0:T(512)(128)(4,1)S(1)} %iota_compare_fusion), kind=kLoop, calls=%fused_computation | loop fusion | flops 524288 | bytes 2097154 | tf_op jit(solution)/shard_map/jit(_where)/select_n | solution.py:449
  (1 shorter events, 0.0 us)

commit v6 on v5

--- a/solution.py
+++ b/solution.py
@@ -10,6 +10,7 @@
 MESH = pl.DeviceIdType.MESH
 LANES = 128
 TAIL = 16
+CUTS = 4
 REACH = 4
 RELAY = True
 F32 = jnp.float32
@@ -399,6 +400,33 @@
     all_sent(grad_sel.at[pl.ds(0, len(far_sides))], back_send.at[0])
     for copy in out_copies(result, out_ref.at[0], out_ref.at[1]):
         copy.wait()
+
+
+def keep_live(counts_ref, in_ref, out_ref, zeros, sem):
+    zeros[...] = jnp.zeros_like(zeros)
+    slots, blocks = in_ref.shape[:2]
+    depth = blocks // CUTS
+
+    def copy(slot, cut, live):
+        place = (slot, pl.ds(cut * depth, depth))
+        source = in_ref.at[place] if live else zeros
+        return pltpu.make_async_copy(source, out_ref.at[place], sem.at[slot, cut])
+
+    for slot in range(slots):
+
+        @pl.when(counts_ref[0] > slot)
+        def _():
+            for cut in range(CUTS):
+                copy(slot, cut, True).start()
+
+        @pl.when(counts_ref[0] <= slot)
+        def _():
+            for cut in range(CUTS):
+                copy(slot, cut, False).start()
+
+    for slot in range(slots):
+        for cut in range(CUTS):
+            copy(slot, cut, True).wait()
 
 
 def on_device(mesh, statistics, gradients, counts):
@@ -445,8 +473,15 @@
         ),
         name="hybrid",
     )(counts, statistics, gradients)
-    live = (jnp.arange(slots) < counts[0])[:, None, None, None]
-    return jnp.where(live, out, jnp.zeros_like(out))
+    return pl.pallas_call(
+        keep_live,
+        out_shape=jax.ShapeDtypeStruct(gradients.shape, BF16),
+        in_specs=[pl.BlockSpec(memory_space=pltpu.SMEM), anywhere],
+        out_specs=anywhere,
+        scratch_shapes=[pltpu.VMEM((blocks // CUTS, height, order), BF16), dma((slots, CUTS))],
+        compiler_params=pltpu.CompilerParams(vmem_limit_bytes=8 * 1024 * 1024),
+        name="keep_live",
+    )(counts, out)
 
 
 def solution(mesh):

time: 59.6 us -> 59.5 us (level)
  other arithmetic: 1.12 us -> 0 us
  Pallas kernels: 57.7 us -> 58.7 us
    select_n x1 -> x0, other arithmetic: 1.11 us -> none  [on_device(): return jnp.where(live, out, jnp.zeros_like(out))]
    pallas_call x0 -> x1, Pallas kernels: none -> 1.04 us  [on_device(): pl.pallas_call(keep_live, out_shape=jax.ShapeDtypeStruct(gradients.shape,...]
where the time goes in v6:
time: 59.5 us; the launch traced here: 59.4 us
  Pallas kernels  58.7 us (99%)
  between operations  0.66 us (1%)
    pallas_call x1, Pallas kernels, on_device(): pl.pallas_call(functools.partial(kernel, ring, reach), out_shape=jax.Shap...  57.7 us

profile of v6, /device:TPU:1, one launch (start us, length us, event | category | flops | bytes accessed | tf_op | source)
XLA Modules:
  0.0 59.4 jit_solution(4125622777538303901)
XLA Ops:
  0.7 57.7 %hybrid.1.in_ref = bf16[2,16,32,512]{3,2,1,0:T(8,128)(2,1)S(1)} custom-call(s32[1]{0:T(128)S(6)} %copy.4.counts_ref, bf16[2,512,512]{2,1,0:T(8,128)(2,1)} %stat_ref.1, bf16[2,16,32,512]{3,2,1,0:T(8,128)(2,1)} %grad_ref.1), custom_call_target="tpu_custom_call" | custom-call | tf_op jit(solution)/shard_map/hybrid/pallas_call | solution.py:443
  58.3 1.0 %keep_live.1 = bf16[2,16,32,512]{3,2,1,0:T(8,128)(2,1)} custom-call(s32[1]{0:T(128)S(6)} %copy.4.counts_ref, bf16[2,16,32,512]{3,2,1,0:T(8,128)(2,1)S(1)} %hybrid.1.in_ref), custom_call_target="tpu_custom_call" | custom-call | tf_op jit(solution)/shard_map/keep_live/pallas_call | solution.py:476

commit v7 on v5

--- a/solution.py
+++ b/solution.py
@@ -324,15 +324,18 @@
     result[me] = apply_root(grad_sel[me], own_root)
     send_out(0)
 
+    def use_here(side, d):
+        offset = d if side else -d
+        result[at(offset)] = apply_root(grad_sel[at(offset)], roots.at[side, d - 1])
+        send_out(offset)
+
     for d in range(1, reach):
         for c in range(chunks):
             for side in range(2):
                 root_copy(side, d, c).wait_recv()
                 root_copy(side, d + 1, c).start()
-        for side in range(2):
-            offset = d if side else -d
-            result[at(offset)] = apply_root(grad_sel[at(offset)], roots.at[side, d - 1])
-            send_out(offset)
+            if d > 1 and c < 2:
+                use_here(c, d - 1)
 
     def back_copy(side, k, part):
         way = 1 if side else -1
@@ -369,6 +372,8 @@
             )
             for k in served[side]:
                 back_copy(side, k, part).start()
+    for side in range(2):
+        use_here(side, reach - 1)
     for side in (1, 0):
         offset = reach if side else -reach
         result[at(offset)] = apply_root(grad_sel[at(offset)], roots.at[side, reach - 1])

time: 59.6 us -> 59.6 us (level)
  no operation moved by 1% of the time
where the time goes in v7:
time: 59.6 us; the launch traced here: 59.4 us
  Pallas kernels  57.7 us (97%)
  other arithmetic  1.12 us (2%)
  between operations  0.67 us (1%)
    pallas_call x1, Pallas kernels, on_device(): pl.pallas_call(functools.partial(kernel, ring, reach), out_shape=jax.Shap...  57.7 us

profile of v7, /device:TPU:1, one launch (start us, length us, event | category | flops | bytes accessed | tf_op | source)
XLA Modules:
  0.0 59.4 jit_solution(3135866596548419214)
XLA Ops:
  0.7 57.7 %hybrid.1 = bf16[2,16,32,512]{3,2,1,0:T(8,128)(2,1)S(1)} custom-call(s32[1]{0:T(128)} %copy.4.counts_ref, bf16[2,512,512]{2,1,0:T(8,128)(2,1)} %stat_ref.1, bf16[2,16,32,512]{3,2,1,0:T(8,128)(2,1)} %grad_ref.1), custom_call_target="tpu_custom_call" | custom-call | tf_op jit(solution)/shard_map/hybrid/pallas_call | solution.py:420
  58.3 1.1 %broadcast_select_fusion = bf16[2,16,32,512]{3,2,1,0:T(8,128)(2,1)} fusion(bf16[2,16,32,512]{3,2,1,0:T(8,128)(2,1)S(1)} %hybrid.1, pred[2]{0:T(512)(128)(4,1)S(1)} %iota_compare_fusion), kind=kLoop, calls=%fused_computation | loop fusion | flops 524288 | bytes 2097154 | tf_op jit(solution)/shard_map/jit(_where)/select_n | solution.py:454
  (1 shorter events, 0.0 us)
